TPU v7x, 256 devices: a whole 4x4x8 slice. The times are simulated.
256 devices in a mesh: snp: 32 (over y, z), ind: 8 (over x, core).
Axes of the slice: x: 4, y: 4, z: 8, core: 2. Of those that a mesh axis runs over, the one named last changes fastest.
Arguments:
- beta_hat: float32 [64, 32768], P('ind', 'snp'), may hold values from -8 to 8
- ld_band: float32 [32768, 1024], P('snp'), as said below
- band_start: int32 [256], P('snp'), may hold values from -480 to 32224, as said below
- heritability: float32 [64], P('ind'), may hold values from 0.2 to 0.6
- genotypes: bfloat16 [8192, 32768], P('ind', 'snp'), may hold values from 0 to 2, as said below
Outputs:
- weights: float32 [64, 32768], P('ind', 'snp')
- scores: float32 [64, 8192], P(None, ('ind', 'snp'))
Inputs may be any that keep to these rules, and one draw needn't show every extreme that they name: ld_band is a symmetric matrix R in band form: entry k of row i is R[i, band_start[i // 128] + k]; R[i, i] = 1; R[i, j] = 0 when |i - j| > 416 or j lies outside the SNPs; the off-diagonal magnitudes of a row sum to 2.5 at most. `band_start`: block b's window starts at 128 * b - 416 - k with k from 0 to 64; the first block has k = 64 and the last block k = 0. `genotypes`: dosages are 0, 1 or 2.
All inputs are finite; a program needn't handle non-finite values.
Results may differ from a plain program's by a relative error of at most 0.0021.
Values may be sent and summed in bfloat16 or wider, within the bound.
A program may use at most 64 MiB of HBM per device.

v0:
```python
import jax
import jax.numpy as jnp
from jax import lax
from jax.sharding import PartitionSpec as P

BLK = 128
ITERS = 2
M_GENOME = 1100000
N_GWAS = 1000000


def padded_2(block, sides, width):
    for axis, dim in sides:
        count = lax.axis_size(axis)
        forward = [(i, i + 1) for i in range(count - 1)]
        backward = [(target, source) for source, target in forward]
        low = lax.ppermute(
            lax.slice_in_dim(block, block.shape[dim] - width, None, axis=dim), axis, forward
        )
        high = lax.ppermute(lax.slice_in_dim(block, 0, width, axis=dim), axis, backward)
        block = jnp.concatenate([low, block, high], axis=dim)
    return block


def apply_operator(vector, ld_band, band_start, ridge_shift):
    band_cols = ld_band.shape[1]
    halo_cols = band_cols - BLK
    padded = padded_2(vector, (("snp", 1),), halo_cols)
    local_rows = vector.shape[1]
    offsets = band_start - lax.axis_index("snp") * local_rows + halo_cols
    windows = jax.vmap(lambda row_begin: lax.dynamic_slice_in_dim(padded, row_begin, band_cols, 1))(
        offsets
    )
    blocks = ld_band.reshape(band_start.shape[0], BLK, band_cols)
    product = jnp.einsum("btk,brk->tbr", windows, blocks, precision=lax.Precision.HIGHEST)
    return product.reshape(vector.shape) + ridge_shift[:, None] * vector


def norm_sum(residual):
    return lax.psum(jnp.sum(residual * residual, axis=1), "snp")


def local(beta_hat, ld_band, band_start, heritability, genotypes):
    ridge_shift = M_GENOME / N_GWAS / heritability
    weights = jnp.zeros_like(beta_hat)
    residual = beta_hat
    direction = beta_hat
    norm_now = norm_sum(residual)
    for turn_index in range(ITERS):
        product = apply_operator(direction, ld_band, band_start, ridge_shift)
        curved = lax.psum(jnp.sum(direction * product, axis=1), "snp")
        step_size = norm_now / curved
        weights = weights + step_size[:, None] * direction
        residual = residual - step_size[:, None] * product
        if turn_index + 1 < ITERS:
            norm_next = norm_sum(residual)
            direction = residual + (norm_next / norm_now)[:, None] * direction
            norm_now = norm_next
    rounded = weights.astype(jnp.bfloat16)
    partial_scores = lax.dot_general(
        lax.all_gather(rounded, "ind", axis=0, tiled=True),
        genotypes,
        (((1,), (1,)), ((), ())),
        preferred_element_type=jnp.float32,
    )
    complete = lax.psum(partial_scores, "snp")
    count = complete.shape[1] * lax.axis_size("ind")
    summed = lax.psum(jnp.sum(complete, axis=1), "ind")
    average = summed / count
    centred = complete - average[:, None]
    variance = lax.psum(jnp.sum(centred * centred, axis=1), "ind") / count
    share_cols = complete.shape[1] // lax.axis_size("snp")
    own_part = lax.dynamic_slice_in_dim(centred, lax.axis_index("snp") * share_cols, share_cols, 1)
    scores = own_part * lax.rsqrt(variance + 1e-05)[:, None]
    return (weights, scores)


def solution(mesh):
    placed = (P("ind", "snp"), P("snp", None), P("snp"), P("ind"), P("ind", "snp"))
    return jax.shard_map(
        local,
        mesh=mesh,
        in_specs=placed,
        out_specs=(P("ind", "snp"), P(None, ("ind", "snp"))),
        check_vma=False,
    )
```

profile of v0, /device:TPU:1, one launch (start us, length us, event | category | flops | bytes accessed | tf_op | source)
XLA Modules:
  0.0 465.0 jit_solution(3514487914134571717)
XLA Ops:
  7.2 0.9 fusion.7
  8.1 4.4 collective-permute-start
  12.5 1.3 collective-permute-start.1
  13.8 0.7 broadcast_divide_fusion
  14.5 0.7 fusion.4
  15.2 2.2 collective-permute-done.1
  17.3 0.8 pad_maximum_fusion
  18.1 10.5 %while.2 = (s32[]{:T(128)}, f32[8,2816]{1,0:T(8,128)S(1)}, s32[8,2]{0,1:T(2,128)S(1)}, f32[8,8,1024]{2,1,0:T(8,128)S(1)}, s32[]{:T(128)}) while((s32[]{:T(128)}, f32[8,2816]{1,0:T(8,128)S(1)}, s32[8,2]{0,1:T(2,128)S(1)}, f32[8,8,1024]{2,1,0:T(8,128)S(1)}, s32[]{:T(128)}) %tuple.38), condition=%wide.while_cond, body=%wide.while_body.sunk | while | flops 2 | bytes 65633 | solution.py:31
  18.7 0.7 bitcast_dynamic-update-slice_fusion.4
  19.5 0.5 slice.46
  20.0 0.7 bitcast_dynamic-update-slice_fusion.4
  21.3 0.7 bitcast_dynamic-update-slice_fusion.4
  22.7 0.7 bitcast_dynamic-update-slice_fusion.4
  24.0 0.7 bitcast_dynamic-update-slice_fusion.4
  24.8 0.5 slice.46
  25.3 0.7 bitcast_dynamic-update-slice_fusion.4
  26.1 0.5 slice.46
  26.6 0.7 bitcast_dynamic-update-slice_fusion.4
  27.9 0.7 bitcast_dynamic-update-slice_fusion.4
  28.6 5.4 %multiply_reduce_fusion.2 = (f32[8]{0:T(128)S(1)}, f32[8]{0:T(128)S(1)}, f32[8,1024]{1,0:T(8,128)S(1)}) fusion(f32[8,1024]{1,0:T(8,128)} %param.5, f32[8]{0:T(128)S(1)} %broadcast_divide_fusion, f32[8,8,1024]{2,1,0:T(8,128)S(1)} %get-tuple-element.9, f32[8,128,1024]{2,1,0:T(8,128)} %bitcast.39), kind=kOutput, calls=%fused_computation.19 | convolution fusion | flops 100712432 | bytes 4522080 | tf_op jit(solution)/shard_map/btk,brk->tbr/dot_general | solution.py:35
  34.1 62.4 %all-reduce.1 = (f32[8]{0:T(128)S(1)}, f32[8]{0:T(128)S(1)}) all-reduce(f32[8]{0:T(128)S(1)} %get-tuple-element.21, f32[8]{0:T(128)S(1)} %get-tuple-element.20), channel_id=1, replica_groups=mesh['snp'=32,'ind'=8] {'snp'}, use_global_device_ids=true, to_apply=%region_1.0 | all-reduce | flops 16 | bytes 128 | tf_op jit(solution)/shard_map/psum | solution.py:40
  96.6 55.7 %psum.51 = f32[8]{0:T(128)S(1)} all-reduce(f32[8]{0:T(128)S(1)} %multiply_reduce_fusion.1), channel_id=1, replica_groups=mesh['snp'=32,'ind'=8] {'snp'}, use_global_device_ids=true, to_apply=%region_5.0 | all-reduce | flops 8 | bytes 64 | tf_op jit(solution)/shard_map/psum | solution.py:40
  152.5 3.6 collective-permute-start.2
  156.0 1.3 collective-permute-start.3
  157.3 3.6 collective-permute-done.3
  161.0 10.5 %while.3 = (s32[]{:T(128)}, f32[8,2816]{1,0:T(8,128)S(1)}, s32[8,2]{0,1:T(2,128)S(1)}, f32[8,8,1024]{2,1,0:T(8,128)S(1)}, s32[]{:T(128)}) while((s32[]{:T(128)}, f32[8,2816]{1,0:T(8,128)S(1)}, s32[8,2]{0,1:T(2,128)S(1)}, f32[8,8,1024]{2,1,0:T(8,128)S(1)}, s32[]{:T(128)}) %tuple.46), condition=%wide.while_cond.1, body=%wide.while_body.1.sunk | while | flops 2 | bytes 65633 | solution.py:31
  161.6 0.7 bitcast_dynamic-update-slice_fusion.5
  162.4 0.5 slice.47
  162.9 0.7 bitcast_dynamic-update-slice_fusion.5
  164.2 0.7 bitcast_dynamic-update-slice_fusion.5
  165.5 0.7 bitcast_dynamic-update-slice_fusion.5
  166.8 0.7 bitcast_dynamic-update-slice_fusion.5
  168.1 0.7 bitcast_dynamic-update-slice_fusion.5
  168.9 0.5 slice.47
  169.5 0.7 bitcast_dynamic-update-slice_fusion.5
  170.3 0.5 slice.47
  170.8 0.7 bitcast_dynamic-update-slice_fusion.5
  171.5 5.4 %fusion.3 = f32[8]{0:T(128)S(1)} fusion(f32[8,1024]{1,0:T(8,128)S(1)} %multiply_add_fusion.1, f32[8,8,1024]{2,1,0:T(8,128)S(1)} %get-tuple-element.17, f32[8,128,1024]{2,1,0:T(8,128)} %bitcast.40, f32[8]{0:T(128)S(1)} %broadcast_divide_fusion), kind=kOutput, calls=%fused_computation.9 | convolution fusion | flops 100696056 | bytes 4489280 | tf_op jit(solution)/shard_map/btk,brk->tbr/dot_general | solution.py:35
  176.9 55.7 %psum.52 = f32[8]{0:T(128)S(1)} all-reduce(f32[8]{0:T(128)S(1)} %fusion.3), channel_id=1, replica_groups=mesh['snp'=32,'ind'=8] {'snp'}, use_global_device_ids=true, to_apply=%region_7.0 | all-reduce | flops 8 | bytes 64 | tf_op jit(solution)/shard_map/psum | solution.py:51
  232.6 0.7 fusion.5
  233.3 57.2 %all_gather.3 = bf16[64,1024]{1,0:T(8,128)(2,1)S(1)} all-gather(bf16[8,1024]{1,0:T(8,128)(2,1)S(1)} %get-tuple-element.42), channel_id=1, replica_groups=mesh['snp'=32,'ind'=8] {'ind'}, dimensions={0}, use_global_device_ids=true | all-gather | bytes 147456 | tf_op jit(solution)/shard_map/all_gather | solution.py:61
  290.5 1.5 fusion.8
  292.0 133.9 %all-reduce.4.cloned.1.call-done = f32[64,1024]{1,0:T(8,128)} async-done(((f32[64,1024]{1,0:T(8,128)}), f32[64,1024]{1,0:T(8,128)}) %all-reduce.4.cloned.1.call-update) | async-done | bytes 262160 | tf_op jit(solution)/shard_map/psum | solution.py:66
  425.9 1.1 reduce_sum.58
  426.9 16.9 %psum.54 = f32[64]{0:T(128)S(1)} all-reduce(f32[64]{0:T(128)S(1)} %reduce_sum.58), channel_id=1, replica_groups=mesh['snp'=32,'ind'=8] {'ind'}, use_global_device_ids=true, to_apply=%region_10.0 | all-reduce | flops 64 | bytes 512 | tf_op jit(solution)/shard_map/psum | solution.py:68
  443.8 1.1 multiply_reduce_fusion
  445.0 12.4 %psum.55 = f32[64]{0:T(128)S(1)} all-reduce(f32[64]{0:T(128)S(1)} %get-tuple-element.40), channel_id=1, replica_groups=mesh['snp'=32,'ind'=8] {'ind'}, use_global_device_ids=true, to_apply=%region_12.0 | all-reduce | flops 64 | bytes 512 | tf_op jit(solution)/shard_map/psum | solution.py:71
  457.5 0.7 copy.7
  (47 shorter events, 6.9 us)
Async XLA Ops:
  7.2 283.4 %copy-start = (bf16[1024,1024]{1,0:T(8,128)(2,1)S(1)}, bf16[1024,1024]{1,0:T(8,128)(2,1)}, u32[]{:S(2)}) copy-start(bf16[1024,1024]{1,0:T(8,128)(2,1)} %param.9) | copy-start | bytes 6291460
  7.2 89.3 %copy-start.1 = (f32[8,1024]{1,0:T(8,128)S(1)}, f32[8,1024]{1,0:T(8,128)}, u32[]{:S(2)}) copy-start(f32[8,1024]{1,0:T(8,128)} %param.5) | copy-start | bytes 98308
  7.2 418.7 %all-reduce.4.cloned.1.call-start = ((), (), s32[]{:S(2)}) async-start(), calls=%async_computation | async-start | bytes 524288 | tf_op jit(solution)/shard_map/psum | solution.py:66
  8.1 7.0 %collective-permute-start = (f32[8,896]{1,0:T(8,128)S(1)}, f32[8,896]{1,0:T(8,128)S(1)}, u32[]{:S(2)}, u32[]{:S(2)}) collective-permute-start(f32[8,896]{1,0:T(8,128)S(1)} %get-tuple-element.46), channel_id=1, source_target_pairs={{0,8},{8,16},{16,24},{24,32},{32,40},{40,48},{48,56},{56,64},{64,7... | collective-permute-start | bytes 86024 | tf_op jit(solution)/shard_map/ppermute | solution.py:17
  12.5 4.8 %collective-permute-start.1 = (f32[8,896]{1,0:T(8,128)S(1)}, f32[8,896]{1,0:T(8,128)S(1)}, u32[]{:S(2)}, u32[]{:S(2)}) collective-permute-start(f32[8,896]{1,0:T(8,128)S(1)} %get-tuple-element.47), channel_id=1, source_target_pairs={{8,0},{16,8},{24,16},{32,24},{40,32},{48,40},{56,48},{64,56},{72,6... | collective-permute-start | bytes 86024 | tf_op jit(solution)/shard_map/ppermute | solution.py:20
  152.5 4.9 %collective-permute-start.2 = (f32[8,896]{1,0:T(8,128)S(1)}, f32[8,896]{1,0:T(8,128)S(1)}, u32[]{:S(2)}, u32[]{:S(2)}) collective-permute-start(f32[8,896]{1,0:T(8,128)S(1)} %get-tuple-element.44), channel_id=1, source_target_pairs={{0,8},{8,16},{16,24},{24,32},{32,40},{40,48},{48,56},{56,64},{64,7... | collective-permute-start | bytes 86024 | tf_op jit(solution)/shard_map/ppermute | solution.py:17
  156.0 4.9 %collective-permute-start.3 = (f32[8,896]{1,0:T(8,128)S(1)}, f32[8,896]{1,0:T(8,128)S(1)}, u32[]{:S(2)}, u32[]{:S(2)}) collective-permute-start(f32[8,896]{1,0:T(8,128)S(1)} %get-tuple-element.45), channel_id=1, source_target_pairs={{8,0},{16,8},{24,16},{32,24},{40,32},{48,40},{56,48},{64,56},{72,6... | collective-permute-start | bytes 86024 | tf_op jit(solution)/shard_map/ppermute | solution.py:20
Sparse Core Ops, SparseCore 0:
  292.1 133.6 all-reduce.3
where the time goes:
time: 466 us; the launch traced here: 465 us
  blocking collectives  260 us (56%)
  waiting for transfers between devices  140 us (30%)
  local copies, waits for them, and re-layouts  22.7 us (5%)
  between operations  14.1 us (3%)
  matrix products  12.3 us (3%)
  starting transfers between devices  10.5 us (2%)
  other arithmetic  5.4 us (1%)
    psum x1, waiting for transfers between devices, local(): complete = lax.psum(partial_scores, 'snp')  134 us
    psum x2, blocking collectives, norm_sum(): return lax.psum(jnp.sum(residual * residual, axis=1), 'snp')  118 us
    all_gather x1, blocking collectives, local(): lax.all_gather(rounded, 'ind', axis=0, tiled=True)  57.2 us
    psum x1, blocking collectives, local(): curved = lax.psum(jnp.sum(direction * product, axis=1), 'snp')  55.7 us
    gather x48, local copies, waits for them, and re-layouts  21 us
    psum x1, blocking collectives, local(): summed = lax.psum(jnp.sum(complete, axis=1), 'ind')  16.9 us
    psum x1, blocking collectives, local(): variance = lax.psum(jnp.sum(centred * centred, axis=1), 'ind') / count  12.4 us
    dot_general x2, matrix products, apply_operator(): jnp.einsum('btk,brk->tbr', windows, blocks, precision=lax.Precision.HIGHEST)  10.8 us
  transfers between devices with their start and end apart: 5, of which 3 were waited for; matrix products, arithmetic and copies ran while one was open for 0% of the time, Pallas kernels for 0%

commit v1 on v0

--- a/solution.py
+++ b/solution.py
@@ -63,7 +63,9 @@
         (((1,), (1,)), ((), ())),
         preferred_element_type=jnp.float32,
     )
-    complete = lax.psum(partial_scores, "snp")
+    complete = partial_scores
+    for hop in (1, 2, 4, 8, 16):
+        complete = complete + lax.ppermute(complete, "snp", [(dev, dev ^ hop) for dev in range(32)])
     count = complete.shape[1] * lax.axis_size("ind")
     summed = lax.psum(jnp.sum(complete, axis=1), "ind")
     average = summed / count

time: 466 us -> 365 us (0.78)
  waiting for transfers between devices: 140 us -> 51.1 us
  between operations: 14.1 us -> 0.79 us
    psum x1 -> x0, waiting for transfers between devices: 134 us -> none  [local(): complete = lax.psum(partial_scores, 'snp')]
    ppermute x0 -> x5, waiting for transfers between devices: none -> 45.3 us  [local(): lax.ppermute(complete, 'snp', [(dev, dev ^ hop) for dev in range(32)])]
  transfers between devices with their start and end apart: 5 -> 9, of which waited for: 3 -> 7; matrix products, arithmetic and copies ran while one was open for 0% -> 0% of each run, Pallas kernels for 0% -> 0%
where the time goes in v1:
time: 365 us; the launch traced here: 364 us
  blocking collectives  262 us (72%)
  waiting for transfers between devices  51.1 us (14%)
  local copies, waits for them, and re-layouts  22.7 us (6%)
  starting transfers between devices  12.7 us (3%)
  matrix products  11.5 us (3%)
    psum x2, blocking collectives, norm_sum(): return lax.psum(jnp.sum(residual * residual, axis=1), 'snp')  118 us
    all_gather x1, blocking collectives, local(): lax.all_gather(rounded, 'ind', axis=0, tiled=True)  57.2 us
    psum x1, blocking collectives, local(): curved = lax.psum(jnp.sum(direction * product, axis=1), 'snp')  55.7 us
    ppermute x5, waiting for transfers between devices, local(): lax.ppermute(complete, 'snp', [(dev, dev ^ hop) for dev in range(32)])  45.3 us
    gather x48, local copies, waits for them, and re-layouts  21 us
    psum x1, blocking collectives, local(): summed = lax.psum(jnp.sum(complete, axis=1), 'ind')  18.1 us
    psum x1, blocking collectives, local(): variance = lax.psum(jnp.sum(centred * centred, axis=1), 'ind') / count  12.4 us
    dot_general x2, matrix products, apply_operator(): jnp.einsum('btk,brk->tbr', windows, blocks, precision=lax.Precision.HIGHEST)  10.8 us
  transfers between devices with their start and end apart: 9, of which 7 were waited for; matrix products, arithmetic and copies ran while one was open for 0% of the time, Pallas kernels for 0%

profile of v1, /device:TPU:1, one launch (start us, length us, event | category | flops | bytes accessed | tf_op | source)
XLA Modules:
  0.0 364.0 jit_solution(7635444210098882748)
XLA Ops:
  0.7 0.9 fusion.8
  1.6 4.4 %collective-permute-start = (f32[8,896]{1,0:T(8,128)S(1)}, f32[8,896]{1,0:T(8,128)S(1)}, u32[]{:S(2)}, u32[]{:S(2)}) collective-permute-start(f32[8,896]{1,0:T(8,128)S(1)} %get-tuple-element.48), channel_id=1, source_target_pairs={{0,8},{8,16},{16,24},{24,32},{32,40},{40,48},{48,56},{56,64},{64,7... | collective-permute-start | bytes 86024 | tf_op jit(solution)/shard_map/ppermute | solution.py:17
  5.9 1.3 collective-permute-start.1
  7.3 0.7 broadcast_divide_fusion
  7.9 0.7 fusion.4
  8.6 2.2 collective-permute-done.1
  10.7 0.8 pad_maximum_fusion
  11.5 10.5 %while.2 = (s32[]{:T(128)}, f32[8,2816]{1,0:T(8,128)S(1)}, s32[8,2]{0,1:T(2,128)S(1)}, f32[8,8,1024]{2,1,0:T(8,128)S(1)}, s32[]{:T(128)}) while((s32[]{:T(128)}, f32[8,2816]{1,0:T(8,128)S(1)}, s32[8,2]{0,1:T(2,128)S(1)}, f32[8,8,1024]{2,1,0:T(8,128)S(1)}, s32[]{:T(128)}) %tuple.39), condition=%wide.while_cond, body=%wide.while_body.sunk | while | flops 2 | bytes 65641 | solution.py:31
  12.1 0.7 bitcast_dynamic-update-slice_fusion.4
  13.5 0.7 bitcast_dynamic-update-slice_fusion.4
  14.8 0.7 bitcast_dynamic-update-slice_fusion.4
  15.6 0.5 slice.46
  16.1 0.7 bitcast_dynamic-update-slice_fusion.4
  16.9 0.5 slice.46
  17.4 0.7 bitcast_dynamic-update-slice_fusion.4
  18.2 0.5 slice.46
  18.7 0.7 bitcast_dynamic-update-slice_fusion.4
  20.0 0.7 bitcast_dynamic-update-slice_fusion.4
  21.3 0.7 bitcast_dynamic-update-slice_fusion.4
  22.1 5.4 %multiply_reduce_fusion.2 = (f32[8]{0:T(128)S(1)}, f32[8]{0:T(128)S(1)}, f32[8,1024]{1,0:T(8,128)S(1)}) fusion(f32[8,1024]{1,0:T(8,128)} %param.5, f32[8]{0:T(128)S(1)} %broadcast_divide_fusion, f32[8,8,1024]{2,1,0:T(8,128)S(1)} %get-tuple-element.9, f32[8,128,1024]{2,1,0:T(8,128)} %bitcast.39), kind=kOutput, calls=%fused_computation.19 | convolution fusion | flops 100712432 | bytes 4522080 | tf_op jit(solution)/shard_map/btk,brk->tbr/dot_general | solution.py:35
  27.5 62.4 %all-reduce.1 = (f32[8]{0:T(128)S(1)}, f32[8]{0:T(128)S(1)}) all-reduce(f32[8]{0:T(128)S(1)} %get-tuple-element.21, f32[8]{0:T(128)S(1)} %get-tuple-element.20), channel_id=1, replica_groups=mesh['snp'=32,'ind'=8] {'snp'}, use_global_device_ids=true, to_apply=%region_1.0 | all-reduce | flops 16 | bytes 128 | tf_op jit(solution)/shard_map/psum | solution.py:40
  90.1 55.7 %psum.44 = f32[8]{0:T(128)S(1)} all-reduce(f32[8]{0:T(128)S(1)} %multiply_reduce_fusion.1), channel_id=1, replica_groups=mesh['snp'=32,'ind'=8] {'snp'}, use_global_device_ids=true, to_apply=%region_5.0 | all-reduce | flops 8 | bytes 64 | tf_op jit(solution)/shard_map/psum | solution.py:40
  145.9 3.6 collective-permute-start.2
  149.5 1.3 collective-permute-start.3
  150.8 3.6 collective-permute-done.3
  154.4 10.5 %while.3 = (s32[]{:T(128)}, f32[8,2816]{1,0:T(8,128)S(1)}, s32[8,2]{0,1:T(2,128)S(1)}, f32[8,8,1024]{2,1,0:T(8,128)S(1)}, s32[]{:T(128)}) while((s32[]{:T(128)}, f32[8,2816]{1,0:T(8,128)S(1)}, s32[8,2]{0,1:T(2,128)S(1)}, f32[8,8,1024]{2,1,0:T(8,128)S(1)}, s32[]{:T(128)}) %tuple.45), condition=%wide.while_cond.1, body=%wide.while_body.1.sunk | while | flops 2 | bytes 65641 | solution.py:31
  155.0 0.7 bitcast_dynamic-update-slice_fusion.5
  156.3 0.7 bitcast_dynamic-update-slice_fusion.5
  157.6 0.7 bitcast_dynamic-update-slice_fusion.5
  159.0 0.7 bitcast_dynamic-update-slice_fusion.5
  160.3 0.7 bitcast_dynamic-update-slice_fusion.5
  161.6 0.7 bitcast_dynamic-update-slice_fusion.5
  162.9 0.7 bitcast_dynamic-update-slice_fusion.5
  164.2 0.7 bitcast_dynamic-update-slice_fusion.5
  164.9 5.4 %fusion.3 = f32[8]{0:T(128)S(1)} fusion(f32[8,1024]{1,0:T(8,128)S(1)} %multiply_add_fusion.1, f32[8,8,1024]{2,1,0:T(8,128)S(1)} %get-tuple-element.17, f32[8,128,1024]{2,1,0:T(8,128)} %bitcast.40, f32[8]{0:T(128)S(1)} %broadcast_divide_fusion), kind=kOutput, calls=%fused_computation.9 | convolution fusion | flops 100696056 | bytes 4489280 | tf_op jit(solution)/shard_map/btk,brk->tbr/dot_general | solution.py:35
  170.3 55.7 %psum.45 = f32[8]{0:T(128)S(1)} all-reduce(f32[8]{0:T(128)S(1)} %fusion.3), channel_id=1, replica_groups=mesh['snp'=32,'ind'=8] {'snp'}, use_global_device_ids=true, to_apply=%region_7.0 | all-reduce | flops 8 | bytes 64 | tf_op jit(solution)/shard_map/psum | solution.py:51
  226.0 0.7 fusion.6
  226.7 57.2 %all_gather.3 = bf16[64,1024]{1,0:T(8,128)(2,1)S(1)} all-gather(bf16[8,1024]{1,0:T(8,128)(2,1)S(1)} %get-tuple-element.44), channel_id=1, replica_groups=mesh['snp'=32,'ind'=8] {'ind'}, dimensions={0}, use_global_device_ids=true | all-gather | bytes 147456 | tf_op jit(solution)/shard_map/all_gather | solution.py:61
  284.0 0.8 fusion.9
  284.7 1.8 collective-permute-start.4
  286.5 6.6 %collective-permute-done.4 = f32[64,1024]{1,0:T(8,128)S(1)} collective-permute-done((f32[64,1024]{1,0:T(8,128)S(1)}, f32[64,1024]{1,0:T(8,128)S(1)}, u32[]{:S(2)}, u32[]{:S(2)}) %collective-permute-start.4) | collective-permute-done | bytes 262176 | tf_op jit(solution)/shard_map/ppermute | solution.py:68
  293.2 13.8 %collective-permute-done.5 = f32[64,1024]{1,0:T(8,128)S(1)} collective-permute-done((f32[64,1024]{1,0:T(8,128)S(1)}, f32[64,1024]{1,0:T(8,128)S(1)}, u32[]{:S(2)}, u32[]{:S(2)}) %collective-permute-start.5) | collective-permute-done | bytes 262176 | tf_op jit(solution)/shard_map/ppermute | solution.py:68
  307.2 13.0 %collective-permute-done.6 = f32[64,1024]{1,0:T(8,128)S(1)} collective-permute-done((f32[64,1024]{1,0:T(8,128)S(1)}, f32[64,1024]{1,0:T(8,128)S(1)}, u32[]{:S(2)}, u32[]{:S(2)}) %collective-permute-start.6) | collective-permute-done | bytes 262176 | tf_op jit(solution)/shard_map/ppermute | solution.py:68
  320.3 5.2 %collective-permute-done.7 = f32[64,1024]{1,0:T(8,128)S(1)} collective-permute-done((f32[64,1024]{1,0:T(8,128)S(1)}, f32[64,1024]{1,0:T(8,128)S(1)}, u32[]{:S(2)}, u32[]{:S(2)}) %collective-permute-start.7) | collective-permute-done | bytes 262176 | tf_op jit(solution)/shard_map/ppermute | solution.py:68
  325.7 6.7 %collective-permute-done.8 = f32[64,1024]{1,0:T(8,128)S(1)} collective-permute-done((f32[64,1024]{1,0:T(8,128)S(1)}, f32[64,1024]{1,0:T(8,128)S(1)}, u32[]{:S(2)}, u32[]{:S(2)}) %collective-permute-start.8) | collective-permute-done | bytes 262176 | tf_op jit(solution)/shard_map/ppermute | solution.py:68
  332.5 18.1 %psum.46 = f32[64]{0:T(128)S(1)} all-reduce(f32[64]{0:T(128)S(1)} %get-tuple-element.42), channel_id=1, replica_groups=mesh['snp'=32,'ind'=8] {'ind'}, use_global_device_ids=true, to_apply=%region_9.0 | all-reduce | flops 64 | bytes 512 | tf_op jit(solution)/shard_map/psum | solution.py:70
  350.8 12.4 %psum.47 = f32[64]{0:T(128)S(1)} all-reduce(f32[64]{0:T(128)S(1)} %get-tuple-element.40), channel_id=1, replica_groups=mesh['snp'=32,'ind'=8] {'ind'}, use_global_device_ids=true, to_apply=%region_11.0 | all-reduce | flops 64 | bytes 512 | tf_op jit(solution)/shard_map/psum | solution.py:73
  363.3 0.7 copy.7
  (58 shorter events, 9.2 us)
Async XLA Ops:
  0.6 283.3 %copy-start = (bf16[1024,1024]{1,0:T(8,128)(2,1)S(1)}, bf16[1024,1024]{1,0:T(8,128)(2,1)}, u32[]{:S(2)}) copy-start(bf16[1024,1024]{1,0:T(8,128)(2,1)} %param.9) | copy-start | bytes 6291460
  0.6 89.2 %copy-start.1 = (f32[8,1024]{1,0:T(8,128)S(1)}, f32[8,1024]{1,0:T(8,128)}, u32[]{:S(2)}) copy-start(f32[8,1024]{1,0:T(8,128)} %param.5) | copy-start | bytes 98308
  1.6 7.0 %collective-permute-start = (f32[8,896]{1,0:T(8,128)S(1)}, f32[8,896]{1,0:T(8,128)S(1)}, u32[]{:S(2)}, u32[]{:S(2)}) collective-permute-start(f32[8,896]{1,0:T(8,128)S(1)} %get-tuple-element.48), channel_id=1, source_target_pairs={{0,8},{8,16},{16,24},{24,32},{32,40},{40,48},{48,56},{56,64},{64,7... | collective-permute-start | bytes 86024 | tf_op jit(solution)/shard_map/ppermute | solution.py:17
  5.9 4.8 %collective-permute-start.1 = (f32[8,896]{1,0:T(8,128)S(1)}, f32[8,896]{1,0:T(8,128)S(1)}, u32[]{:S(2)}, u32[]{:S(2)}) collective-permute-start(f32[8,896]{1,0:T(8,128)S(1)} %get-tuple-element.49), channel_id=1, source_target_pairs={{8,0},{16,8},{24,16},{32,24},{40,32},{48,40},{56,48},{64,56},{72,6... | collective-permute-start | bytes 86024 | tf_op jit(solution)/shard_map/ppermute | solution.py:20
  145.9 4.9 %collective-permute-start.2 = (f32[8,896]{1,0:T(8,128)S(1)}, f32[8,896]{1,0:T(8,128)S(1)}, u32[]{:S(2)}, u32[]{:S(2)}) collective-permute-start(f32[8,896]{1,0:T(8,128)S(1)} %get-tuple-element.46), channel_id=1, source_target_pairs={{0,8},{8,16},{16,24},{24,32},{32,40},{40,48},{48,56},{56,64},{64,7... | collective-permute-start | bytes 86024 | tf_op jit(solution)/shard_map/ppermute | solution.py:17
  149.5 4.9 %collective-permute-start.3 = (f32[8,896]{1,0:T(8,128)S(1)}, f32[8,896]{1,0:T(8,128)S(1)}, u32[]{:S(2)}, u32[]{:S(2)}) collective-permute-start(f32[8,896]{1,0:T(8,128)S(1)} %get-tuple-element.47), channel_id=1, source_target_pairs={{8,0},{16,8},{24,16},{32,24},{40,32},{48,40},{56,48},{64,56},{72,6... | collective-permute-start | bytes 86024 | tf_op jit(solution)/shard_map/ppermute | solution.py:20
  284.7 8.4 %collective-permute-start.4 = (f32[64,1024]{1,0:T(8,128)S(1)}, f32[64,1024]{1,0:T(8,128)S(1)}, u32[]{:S(2)}, u32[]{:S(2)}) collective-permute-start(f32[64,1024]{1,0:T(8,128)S(1)} %fusion.9), channel_id=1, source_target_pairs={{0,8},{8,0},{16,24},{24,16},{32,40},{40,32},{48,56},{56,48},{64,72... | collective-permute-start | bytes 786440 | tf_op jit(solution)/shard_map/ppermute | solution.py:68
  293.1 13.9 %collective-permute-start.5 = (f32[64,1024]{1,0:T(8,128)S(1)}, f32[64,1024]{1,0:T(8,128)S(1)}, u32[]{:S(2)}, u32[]{:S(2)}) collective-permute-start(f32[64,1024]{1,0:T(8,128)S(1)} %add.69), channel_id=1, source_target_pairs={{0,16},{8,24},{16,0},{24,8},{32,48},{40,56},{48,32},{56,40},{64,80... | collective-permute-start | bytes 786440 | tf_op jit(solution)/shard_map/ppermute | solution.py:68
  307.1 13.1 %collective-permute-start.6 = (f32[64,1024]{1,0:T(8,128)S(1)}, f32[64,1024]{1,0:T(8,128)S(1)}, u32[]{:S(2)}, u32[]{:S(2)}) collective-permute-start(f32[64,1024]{1,0:T(8,128)S(1)} %add.70), channel_id=1, source_target_pairs={{0,32},{8,40},{16,48},{24,56},{32,0},{40,8},{48,16},{56,24},{64,96... | collective-permute-start | bytes 786440 | tf_op jit(solution)/shard_map/ppermute | solution.py:68
  320.2 5.3 %collective-permute-start.7 = (f32[64,1024]{1,0:T(8,128)S(1)}, f32[64,1024]{1,0:T(8,128)S(1)}, u32[]{:S(2)}, u32[]{:S(2)}) collective-permute-start(f32[64,1024]{1,0:T(8,128)S(1)} %add.71), channel_id=1, source_target_pairs={{0,64},{8,72},{16,80},{24,88},{32,96},{40,104},{48,112},{56,120},{... | collective-permute-start | bytes 786440 | tf_op jit(solution)/shard_map/ppermute | solution.py:68
  325.6 6.8 %collective-permute-start.8 = (f32[64,1024]{1,0:T(8,128)S(1)}, f32[64,1024]{1,0:T(8,128)S(1)}, u32[]{:S(2)}, u32[]{:S(2)}) collective-permute-start(f32[64,1024]{1,0:T(8,128)S(1)} %add.72), channel_id=1, source_target_pairs={{0,128},{8,136},{16,144},{24,152},{32,160},{40,168},{48,176},{56,1... | collective-permute-start | bytes 786440 | tf_op jit(solution)/shard_map/ppermute | solution.py:68
